TPU v7x, 32 devices: a whole 2x2x4 slice. The times are simulated.
32 devices in a mesh: seq: 4 (over x, core), chan: 8 (over z, y).
Axes of the slice: x: 2, y: 2, z: 4, core: 2. Of those that a mesh axis runs over, the one named last changes fastest.
Arguments:
- inputs: bfloat16 [768, 262144], P('chan', 'seq'), may hold values from -6 to 6
- kernel: bfloat16 [768, 512, 512], P('chan', 'seq'), may hold values from -6 to 6
- forward_one: bfloat16 [512, 512], replicated, may hold values from -0.25 to 0.25
- forward_two: bfloat16 [512, 512], replicated, may hold values from -0.25 to 0.25
- inverse_one: bfloat16 [512, 512], replicated, may hold values from -0.25 to 0.25
- inverse_two: bfloat16 [512, 512], replicated, may hold values from -0.25 to 0.25
- norm_gain: float32 [768], replicated, may hold values from 0.1 to 1.9
- w_gate: bfloat16 [1536, 768], P('chan'), may hold values from -0.21875 to 0.21875
- w_up: bfloat16 [1536, 768], P('chan'), may hold values from -0.21875 to 0.21875
- w_down: bfloat16 [1536, 768], P('chan'), may hold values from -0.15625 to 0.15625
Outputs:
- output: bfloat16 [768, 262144], P('chan', 'seq')
All inputs are finite; a program needn't handle non-finite values.
Results may differ from a plain program's by a relative error of at most 0.0075.
Values may be sent and summed in bfloat16 or wider, within the bound.
A program may use at most 192 MiB of HBM per device.

v0:
```python
import jax
import jax.numpy as jnp
from jax import lax
from jax.sharding import PartitionSpec as P


def shards(
    inputs,
    kernel,
    forward_one,
    forward_two,
    inverse_one,
    inverse_two,
    norm_gain,
    w_gate,
    w_up,
    w_down,
):
    channels_here = inputs.shape[0]
    block_width = forward_one.shape[0]
    block_rows = inputs.shape[1] // block_width
    cube = inputs.reshape(channels_here, block_rows, block_width)
    first_section = jnp.einsum(
        "cab,bk->cak", cube, forward_one, preferred_element_type=jnp.float32
    ).astype(jnp.bfloat16)
    spectrum = jnp.einsum(
        "cak,aj->ckj",
        lax.all_to_all(first_section, "seq", split_axis=2, concat_axis=1, tiled=True),
        forward_two,
        preferred_element_type=jnp.float32,
    )
    scaled = (spectrum * kernel.astype(jnp.float32)).astype(jnp.bfloat16)
    partial_inv = jnp.einsum(
        "ckj,ji->cki", scaled, inverse_two, preferred_element_type=jnp.float32
    ).astype(jnp.bfloat16)
    mixed_out = jnp.einsum(
        "cki,km->cim",
        lax.all_to_all(partial_inv, "seq", split_axis=2, concat_axis=1, tiled=True),
        inverse_one,
        preferred_element_type=jnp.float32,
    )
    resid = (cube.astype(jnp.float32) + mixed_out).astype(jnp.bfloat16)
    resid = resid.reshape(channels_here, block_rows * block_width)
    tokens = lax.all_to_all(resid, "chan", split_axis=1, concat_axis=0, tiled=True)
    stream = tokens.astype(jnp.float32)
    mean_square = jnp.mean(stream * stream, axis=0, keepdims=True)
    normed = (stream * lax.rsqrt(mean_square + 1e-05) * norm_gain[:, None]).astype(jnp.bfloat16)
    gate_rows = lax.all_gather(w_gate, "chan", axis=0, tiled=True)
    up_rows = lax.all_gather(w_up, "chan", axis=0, tiled=True)
    down_rows = lax.all_gather(w_down, "chan", axis=0, tiled=True)
    gate_part = jnp.dot(gate_rows, normed, preferred_element_type=jnp.float32)
    up_part = jnp.dot(up_rows, normed, preferred_element_type=jnp.float32)
    hidden = (jax.nn.gelu(gate_part, approximate=True) * up_part).astype(jnp.bfloat16)
    summed = lax.dot_general(
        down_rows, hidden, (((0,), (0,)), ((), ())), preferred_element_type=jnp.float32
    )
    result = (stream + summed).astype(jnp.bfloat16)
    return lax.all_to_all(result, "chan", split_axis=0, concat_axis=1, tiled=True)


def solution(mesh):
    return jax.shard_map(
        shards,
        mesh=mesh,
        in_specs=(
            P("chan", "seq"),
            P("chan", "seq", None),
            P(),
            P(),
            P(),
            P(),
            P(),
            P("chan", None),
            P("chan", None),
            P("chan", None),
        ),
        out_specs=P("chan", "seq"),
        check_vma=False,
    )
```

profile of v0, /device:TPU:13, one launch (start us, length us, event | category | flops | bytes accessed | tf_op | source)
XLA Modules:
  0.0 1218.3 jit_solution(17737813234452086773)
XLA Ops:
  6.5 0.0 copy-start
  6.5 9.5 copy.35
  16.0 0.0 copy-start.2
  16.0 4.8 copy-done.2
  20.8 0.0 copy-done
  20.8 9.5 convolution_convert_fusion
  30.3 16.5 %copy.24 = bf16[96,128,512]{1,0,2:T(8,128)(2,1)} copy(bf16[96,128,512]{2,1,0:T(8,128)(2,1)} %convolution_convert_fusion) | data formatting | bytes 25165824 | tf_op jit(solution)/shard_map/convert_element_type | solution.py:25
  46.8 147.0 %all_to_all.68 = bf16[96,128,512]{1,0,2:T(8,128)(2,1)} all-to-all(bf16[96,128,512]{1,0,2:T(8,128)(2,1)} %copy.24), channel_id=1, replica_groups=mesh['seq'=4,'chan'=8] {'seq'}, dimensions={2} | all-to-all | bytes 25165824 | tf_op jit(solution)/shard_map/all_to_all | solution.py:28
  193.8 0.0 copy-start.4
  193.8 0.0 copy-start.5
  193.8 17.6 %copy.26 = bf16[96,4,128,128]{3,2,1,0:T(8,128)(2,1)} copy(bf16[96,4,128,128]{2,0,3,1:T(8,128)(2,1)} %bitcast.69) | data formatting | bytes 25165824 | tf_op jit(solution)/shard_map/all_to_all | solution.py:28
  211.4 0.0 copy-done.4
  211.4 0.0 copy-done.5
  211.4 19.5 %fusion.16 = bf16[96,128,512]{2,1,0:T(8,128)(2,1)} fusion(bf16[96,128,512]{2,1,0:T(8,128)(2,1)} %param.11, bf16[96,512,128]{2,1,0:T(8,128)(2,1)} %bitcast.77, bf16[512,512]{1,0:T(8,128)(2,1)S(1)} %copy-done.4, bf16[512,512]{1,0:T(8,128)(2,1)S(1)} %copy-done.5), kind=kOutput, calls=%fused_computation.22 | convolution fusion | flops 12910067712 | bytes 38797312 | tf_op jit(solution)/shard_map/ckj,ji->cki/dot_general | solution.py:33
  230.9 16.5 %copy.28 = bf16[96,128,512]{1,0,2:T(8,128)(2,1)} copy(bf16[96,128,512]{2,1,0:T(8,128)(2,1)} %fusion.16) | data formatting | bytes 25165824 | tf_op jit(solution)/shard_map/convert_element_type | solution.py:35
  247.5 142.5 %all_to_all.69 = bf16[96,128,512]{1,0,2:T(8,128)(2,1)S(1)} all-to-all(bf16[96,128,512]{1,0,2:T(8,128)(2,1)} %copy.28), channel_id=1, replica_groups=mesh['seq'=4,'chan'=8] {'seq'}, dimensions={2} | all-to-all | bytes 25165824 | tf_op jit(solution)/shard_map/all_to_all | solution.py:38
  389.9 25.2 %copy.37 = bf16[96,128,4,128]{1,2,3,0:T(4,128)(2,1)} copy(bf16[96,128,4,128]{1,0,3,2:T(8,128)(2,1)S(1)} %bitcast.70) | data formatting | bytes 25165824 | tf_op jit(solution)/shard_map/all_to_all | solution.py:38
  415.2 0.0 copy-start.6
  415.2 19.1 %all_to_all.57 = bf16[96,512,128]{1,2,0:T(8,128)(2,1)} reshape(bf16[96,4,128,128]{2,1,3,0:T(4,128)(2,1)} %bitcast.71) | data formatting | bytes 25165824 | tf_op jit(solution)/shard_map/all_to_all | solution.py:38
  434.2 0.0 copy-done.6
  434.2 16.0 %add_convert_fusion = bf16[96,128,512]{2,1,0:T(8,128)(2,1)} fusion(bf16[96,128,512]{2,1,0:T(8,128)(2,1)} %bitcast.75, bf16[96,512,128]{1,2,0:T(8,128)(2,1)} %all_to_all.57, bf16[512,512]{1,0:T(8,128)(2,1)S(1)} %copy-done.6), kind=kOutput, calls=%fused_computation.17 | convolution fusion | flops 6461325312 | bytes 38273024 | tf_op jit(solution)/shard_map/cki,km->cim/dot_general | solution.py:36
  450.3 19.5 %all_to_all.58 = bf16[96,8,8192]{2,1,0:T(8,128)(2,1)} reshape(bf16[96,128,512]{2,1,0:T(8,128)(2,1)} %add_convert_fusion) | data formatting | bytes 25165824 | tf_op jit(solution)/shard_map/all_to_all | solution.py:44
  469.8 14.4 %copy.30 = bf16[96,8,8192]{2,0,1:T(8,128)(2,1)} copy(bf16[96,8,8192]{2,1,0:T(8,128)(2,1)} %all_to_all.58) | data formatting | bytes 25165824 | tf_op jit(solution)/shard_map/all_to_all | solution.py:44
  484.2 5.7 all-to-all-start.2
  489.9 0.0 copy-start.3
  489.9 0.0 all-gather.4.cloned.1.call-start
  489.9 0.7 all-gather.4.cloned.1.call-update
  490.6 0.0 all-gather.6.cloned.1.call-start
  490.6 0.7 all-gather.6.cloned.1.call-update
  491.3 0.3 all-gather.8.cloned.1.call-start
  491.6 0.5 all-gather.8.cloned.1.call-update
  492.1 306.1 %all-to-all-done.2 = bf16[96,8,8192]{2,0,1:T(8,128)(2,1)} async-done(((bf16[96,8,8192]{2,0,1:T(8,128)(2,1)}), bf16[96,8,8192]{2,0,1:T(8,128)(2,1)}, u32[]{:S(2)}, u32[]{:S(2)}) %all-to-all-start.2) | async-done | bytes 12582944 | tf_op jit(solution)/shard_map/all_to_all | solution.py:44
  798.2 7.6 fusion.10
  805.8 0.0 copy-done.3
  805.8 12.2 %fusion.12 = bf16[768,8192]{1,0:T(8,128)(2,1)} fusion(bf16[96,8,8192]{2,0,1:T(8,128)(2,1)} %all-to-all-done.2, f32[768]{0:T(1024)S(1)} %copy-done.3, f32[8192]{0:T(1024)S(1)} %add_rsqrt_fusion), kind=kLoop, calls=%fused_computation.16 | loop fusion | flops 25165824 | bytes 25201664 | tf_op jit(solution)/shard_map/convert_element_type | solution.py:47
  818.1 0.0 all-gather.4.cloned.1.call-done
  818.1 31.3 %fusion.26 = f32[8192,1536]{1,0:T(8,128)} fusion(bf16[768,8192]{1,0:T(8,128)(2,1)} %fusion.12, bf16[1536,768]{1,0:T(8,128)(2,1)} %all-gather.4.cloned.1.call-done), kind=kOutput, calls=%fused_computation.33 | convolution fusion | flops 19327352832 | bytes 65273856 | tf_op jit(solution)/shard_map/dot_general | solution.py:51
  849.4 0.0 all-gather.6.cloned.1.call-done
  849.4 29.9 %all-gather.8.cloned.1.call-done = bf16[1536,768]{1,0:T(8,128)(2,1)} async-done(((bf16[192,768]{1,0:T(8,128)(2,1)}), bf16[1536,768]{1,0:T(8,128)(2,1)}) %all-gather.8.cloned.1.call-update) | async-done | bytes 2359312 | tf_op jit(solution)/shard_map/all_gather | solution.py:50
  879.3 52.7 %fusion.9 = bf16[768,8192]{1,0:T(8,128)(2,1)} fusion(bf16[96,8,8192]{2,0,1:T(8,128)(2,1)} %all-to-all-done.2, bf16[1536,768]{1,0:T(8,128)(2,1)} %all-gather.8.cloned.1.call-done, f32[8192,1536]{1,0:T(8,128)} %fusion.26, bf16[768,8192]{1,0:T(8,128)(2,1)} %fusion.12, bf16[1536,768]{1,0:T(8,128)(2,1)} %all-gather.6.cloned.1.call-done), kind=kOutput, calls=%fused_computation.11 | convolution fusion | flops 38799409152 | bytes 92798976 | tf_op jit(solution)/shard_map/dot_general | solution.py:54
  932.0 274.7 %all_to_all.70 = bf16[8,96,8192]{2,1,0:T(8,128)(2,1)S(1)} all-to-all(bf16[8,96,8192]{2,1,0:T(8,128)(2,1)} %bitcast.76), channel_id=1, replica_groups=mesh['seq'=4,'chan'=8] {'chan'}, dimensions={0} | all-to-all | bytes 25165824 | tf_op jit(solution)/shard_map/all_to_all | solution.py:58
  1206.7 0.0 copy-start.1
  1206.7 5.1 copy.34
  1211.7 0.0 copy-done.1
  (1 shorter events, 0.0 us)
Async XLA Ops:
  6.5 14.2 %copy-start = (bf16[512,512]{1,0:T(8,128)(2,1)S(1)}, bf16[512,512]{1,0:T(8,128)(2,1)}, u32[]{:S(2)}) copy-start(bf16[512,512]{1,0:T(8,128)(2,1)} %param.12) | copy-start | bytes 1572868
  16.0 4.8 copy-start.2
  193.8 17.6 %copy-start.4 = (bf16[512,512]{1,0:T(8,128)(2,1)S(1)}, bf16[512,512]{1,0:T(8,128)(2,1)}, u32[]{:S(2)}) copy-start(bf16[512,512]{1,0:T(8,128)(2,1)} %param.15) | copy-start | bytes 1572868
  193.8 17.6 %copy-start.5 = (bf16[512,512]{1,0:T(8,128)(2,1)S(1)}, bf16[512,512]{1,0:T(8,128)(2,1)}, u32[]{:S(2)}) copy-start(bf16[512,512]{1,0:T(8,128)(2,1)} %param.13) | copy-start | bytes 1572868
  415.2 19.1 %copy-start.6 = (bf16[512,512]{1,0:T(8,128)(2,1)S(1)}, bf16[512,512]{1,0:T(8,128)(2,1)}, u32[]{:S(2)}) copy-start(bf16[512,512]{1,0:T(8,128)(2,1)} %param.14) | copy-start | bytes 1572868
  484.2 314.0 %all-to-all-start.2 = ((bf16[96,8,8192]{2,0,1:T(8,128)(2,1)}), bf16[96,8,8192]{2,0,1:T(8,128)(2,1)}, u32[]{:S(2)}, u32[]{:S(2)}) async-start(bf16[96,8,8192]{2,0,1:T(8,128)(2,1)} %copy.30), calls=%async_computation.2 | async-start | bytes 25165824 | tf_op jit(solution)/shard_map/all_to_all | solution.py:44
  489.9 315.9 %copy-start.3 = (f32[768]{0:T(1024)S(1)}, f32[768]{0:T(1024)}, u32[]{:S(2)}) copy-start(f32[768]{0:T(1024)} %param.16) | copy-start | bytes 9220
  489.9 328.2 %all-gather.4.cloned.1.call-start = ((), (), s32[]{:S(2)}) async-start(), calls=%async_computation.4 | async-start | bytes 2654208 | tf_op jit(solution)/shard_map/all_gather | solution.py:48
  490.6 358.8 %all-gather.6.cloned.1.call-start = ((), (), s32[]{:S(2)}) async-start(), calls=%async_computation.5 | async-start | bytes 2654208 | tf_op jit(solution)/shard_map/all_gather | solution.py:49
  491.3 387.9 %all-gather.8.cloned.1.call-start = ((), (), s32[]{:S(2)}) async-start(), calls=%async_computation.6 | async-start | bytes 2654208 | tf_op jit(solution)/shard_map/all_gather | solution.py:50
  1206.7 5.1 copy-start.1
Sparse Core Ops, SparseCore 0:
  492.9 237.8 all-gather.3
  732.9 93.4 all-gather.5
  828.6 50.6 all-gather.7
where the time goes:
time: 1230 us; the launch traced here: 1220 us
  blocking collectives  564 us (46%)
  waiting for transfers between devices  338 us (27%)
  local copies, waits for them, and re-layouts  148 us (12%)
  matrix products  129 us (10%)
  other arithmetic  19.8 us (2%)
  between operations  13.2 us (1%)
    all_to_all x1, waiting for transfers between devices, shards(): lax.all_to_all(resid, 'chan', split_axis=1, concat_axis=0, tiled=True)  306 us
    all_to_all x1, blocking collectives, shards(): lax.all_to_all(result, 'chan', split_axis=0, concat_axis=1, tiled=True)  275 us
    all_to_all x1, blocking collectives, shards(): lax.all_to_all(first_section, 'seq', split_axis=2, concat_axis=1, tiled=T...  147 us
    all_to_all x1, blocking collectives, shards(): lax.all_to_all(partial_inv, 'seq', split_axis=2, concat_axis=1, tiled=True)  142 us
    dot_general x1, matrix products, shards(): lax.dot_general(down_rows, hidden, (((0,), (0,)), ((), ())), preferred_el...  52.7 us
    all_to_all x2, local copies, waits for them, and re-layouts, shards(): lax.all_to_all(partial_inv, 'seq', split_axis=2, concat_axis=1, tiled=True)  44.3 us
    all_to_all x2, local copies, waits for them, and re-layouts, shards(): lax.all_to_all(resid, 'chan', split_axis=1, concat_axis=0, tiled=True)  33.9 us
    dot_general x1, matrix products, shards(): gate_part = jnp.dot(gate_rows, normed, preferred_element_type=jnp.float32)  31.3 us
  transfers between devices with their start and end apart: 4, of which 2 were waited for; matrix products, arithmetic and copies ran while one was open for 4% of the time, Pallas kernels for 0%

commit v1 on v0

--- a/solution.py
+++ b/solution.py
@@ -1,10 +1,501 @@
+import functools
+
 import jax
 import jax.numpy as jnp
 from jax import lax
+from jax.experimental import pallas as pl
+from jax.experimental.pallas import tpu as pltpu
 from jax.sharding import PartitionSpec as P
 
+MESH = pl.DeviceIdType.MESH
+F32 = jnp.float32
+BF16 = jnp.bfloat16
+ROWS = 16
+
+
+def greet(peers):
+    barrier = pltpu.get_barrier_semaphore()
+    for axis, count in peers:
+        me = lax.axis_index(axis)
+        for r in range(1, count):
+            pl.semaphore_signal(
+                barrier,
+                inc=1,
+                device_id={axis: lax.rem(me + r, count)},
+                device_id_type=MESH,
+            )
+    pl.semaphore_wait(barrier, sum(count - 1 for _, count in peers))
+
+
+def mix_kernel(
+    nseq,
+    nchan,
+    x_hbm,
+    kern_hbm,
+    f1_ref,
+    f2t_ref,
+    i2t_ref,
+    i1_ref,
+    tok_hbm,
+    xbuf,
+    kbuf,
+    send1,
+    recv1,
+    send2,
+    recv2,
+    zbuf,
+    scr1,
+    scr2,
+    xsem,
+    ksem,
+    s1sem,
+    r1sem,
+    s2sem,
+    r2sem,
+    zssem,
+    zrsem,
+):
+    order = f1_ref.shape[0]
+    here = order // nseq
+    per = here // nchan
+    chans = x_hbm.shape[0]
+    chunks = chans // ROWS
+    me_s = lax.axis_index("seq")
+    me_c = lax.axis_index("chan")
+
+    def load_x(n):
+        return pltpu.make_async_copy(
+            x_hbm.at[pl.ds(n * ROWS, ROWS), :], xbuf.at[n % 4], xsem.at[n % 4]
+        )
+
+    def load_k(n):
+        return pltpu.make_async_copy(
+            kern_hbm.at[pl.ds(n * ROWS, ROWS)], kbuf.at[n % 2], ksem.at[n % 2]
+        )
+
+    def across(send, recv, ssem, rsem, n, r):
+        to = lax.rem(me_s + r, nseq)
+        return pltpu.make_async_remote_copy(
+            src_ref=send.at[n % 2, to],
+            dst_ref=recv.at[n % 3, me_s],
+            send_sem=ssem.at[n % 2, r],
+            recv_sem=rsem.at[n % 3, r],
+            device_id={"seq": to},
+            device_id_type=MESH,
+        )
+
+    def arrived(send, recv, ssem, rsem, n, r):
+        source = lax.rem(me_s + nseq - r, nseq)
+        return pltpu.make_async_remote_copy(
+            src_ref=send.at[n % 2, source],
+            dst_ref=recv.at[n % 3, source],
+            send_sem=ssem.at[n % 2, r],
+            recv_sem=rsem.at[n % 3, r],
+            device_id={"seq": source},
+            device_id_type=MESH,
+        )
+
+    def own(send, recv, ssem, n):
+        return pltpu.make_async_copy(
+            send.at[n % 2, me_s], recv.at[n % 3, me_s], ssem.at[n % 2, 0]
+        )
+
+    first = (send1, recv1, s1sem, r1sem)
+    second = (send2, recv2, s2sem, r2sem)
+
+    def start_all(stage, n):
+        for r in range(1, nseq):
+            across(*stage, n, r).start()
+        own(stage[0], stage[1], stage[2], n).start()
+
+    def wait_all(stage, n):
+        own(stage[0], stage[1], stage[2], n).wait()
+        for r in range(1, nseq):
+            arrived(*stage, n, r).wait_recv()
+
+    def wait_sent(stage, n):
+        for r in range(1, nseq):
+            across(*stage, n, r).wait_send()
+
+    def z_copy(n, r):
+        to = lax.rem(me_c + r, nchan)
+        return pltpu.make_async_remote_copy(
+            src_ref=zbuf.at[n % 2, to],
+            dst_ref=tok_hbm.at[pl.ds(me_c * chans + n * ROWS, ROWS), :],
+            send_sem=zssem.at[n % 2, r],
+            recv_sem=zrsem.at[n, r],
+            device_id={"chan": to},
+            device_id_type=MESH,
+        )
+
+    def z_arrived(n, r):
+        source = lax.rem(me_c + nchan - r, nchan)
+        return pltpu.make_async_remote_copy(
+            src_ref=zbuf.at[n % 2, source],
+            dst_ref=tok_hbm.at[pl.ds(source * chans + n * ROWS, ROWS), :],
+            send_sem=zssem.at[n % 2, r],
+            recv_sem=zrsem.at[n, r],
+            device_id={"chan": source},
+            device_id_type=MESH,
+        )
+
+    def z_own(n):
+        return pltpu.make_async_copy(
+            zbuf.at[n % 2, me_c],
+            tok_hbm.at[pl.ds(me_c * chans + n * ROWS, ROWS), :],
+            zssem.at[n % 2, 0],
+        )
+
+    def stage_one(n):
+        def body(g, carry):
+            x = xbuf[n % 4, :, pl.ds(g * (ROWS * order), ROWS * order)]
+            lhs = jnp.concatenate(
+                [x[:, a * order : (a + 1) * order] for a in range(ROWS)], axis=0
+            )
+            out = jnp.dot(lhs, f1_ref[...], preferred_element_type=F32)
+            for d in range(nseq):
+                scr1[d * ROWS * ROWS : (d + 1) * ROWS * ROWS, :] = out[
+                    :, d * here : (d + 1) * here
+                ]
+            for d in range(nseq):
+                for c in range(ROWS):
+                    v = scr1[pl.ds(d * ROWS * ROWS + c, ROWS, stride=ROWS), :]
+                    send1[n % 2, d, c, pl.ds(g * ROWS, ROWS), :] = v.astype(BF16)
+            return carry
+
+        lax.fori_loop(0, here // ROWS, body, 0)
+
+    def stage_two(n):
+        def body(p, carry):
+            c = 2 * p
+            fs = jnp.concatenate(
+                [
+                    jnp.concatenate([recv1[n % 3, s, c + e] for s in range(nseq)], axis=0)
+                    for e in range(2)
+                ],
+                axis=1,
+            )
+            spectrum = jnp.dot(f2t_ref[...], fs, preferred_element_type=F32)
+            kern = jnp.concatenate([kbuf[n % 2, c], kbuf[n % 2, c + 1]], axis=0)
+            scaled = (spectrum * kern.astype(F32).T).astype(BF16)
+            inv = jnp.dot(i2t_ref[...], scaled, preferred_element_type=F32)
+            for e in range(2):
+                scr2[pl.ds(c + e, order, stride=ROWS), :] = inv[:, e * here : (e + 1) * here]
+            return carry
+
+        lax.fori_loop(0, ROWS // 2, body, 0)
+
+        def cast(d, carry):
+            send2[n % 2, d] = scr2[pl.ds(d * (here * ROWS), here * ROWS), :].astype(BF16)
+            return carry
+
+        lax.fori_loop(0, nseq, cast, 0)
+
+    def stage_three(n):
+        def body(step, carry):
+            r = lax.rem(step + 1, nchan)
+            to = lax.rem(me_c + r, nchan)
+
+            @pl.when(jnp.logical_and(n >= 2, r > 0))
+            def _():
+                z_copy(n - 2, r).wait_send()
+
+            @pl.when(jnp.logical_and(n >= 2, r == 0))
+            def _():
+                z_own(n - 2).wait()
+
+            rows = pl.ds(to * (per * ROWS), per * ROWS)
+            lhs = jnp.concatenate([recv2[n % 3, s, rows, :] for s in range(nseq)], axis=1)
+            mixed = jnp.dot(lhs, i1_ref[...], preferred_element_type=F32)
+            x = xbuf[n % 4, :, pl.ds(to * (per * order), per * order)].astype(F32)
+            for i in range(per):
+                cols = slice(i * order, (i + 1) * order)
+                zbuf[n % 2, to, :, cols] = (
+                    x[:, cols] + mixed[i * ROWS : (i + 1) * ROWS]
+                ).astype(BF16)
+
+            @pl.when(r > 0)
+            def _():
+                z_copy(n, r).start()
+
+            @pl.when(r == 0)
+            def _():
+                z_own(n).start()
+
+            return carry
+
+        lax.fori_loop(0, nchan, body, 0)
+
+    load_x(0).start()
+    greet((("seq", nseq), ("chan", nchan)))
+
+    def step(t, carry):
+        @pl.when(t < chunks)
+        def _():
+            @pl.when(t + 1 < chunks)
+            def _():
+                load_x(t + 1).start()
+
+            load_k(t).start()
+            load_x(t).wait()
+
+            @pl.when(t >= 2)
+            def _():
+                wait_sent(first, t - 2)
+
+            stage_one(t)
+            start_all(first, t)
+
+        @pl.when(jnp.logical_and(t >= 1, t - 1 < chunks))
+        def _():
+            n = t - 1
+            load_k(n).wait()
+            wait_all(first, n)
+
+            @pl.when(n >= 2)
+            def _():
+                wait_sent(second, n - 2)
+
+            stage_two(n)
+            start_all(second, n)
+
+        @pl.when(t >= 2)
+        def _():
+            n = t - 2
+            wait_all(second, n)
+            stage_three(n)
+
+        return carry
+
+    lax.fori_loop(0, chunks + 2, step, 0)
+    for n in range(max(chunks - 2, 0), chunks):
+        wait_sent(first, n)
+        wait_sent(second, n)
+        z_own(n).wait()
+        for r in range(1, nchan):
+            z_copy(n, r).wait_send()
+
+    def drain(n, carry):
+        for r in range(1, nchan):
+            z_arrived(n, r).wait_recv()
+        return carry
+
+    lax.fori_loop(0, chunks, drain, 0)
+
+
+def mix(inputs, kernel, forward_one, forward_two, inverse_one, inverse_two, nseq, nchan):
+    chans, here_positions = inputs.shape
+    order = forward_one.shape[0]
+    here = order // nseq
+    chunks = chans // ROWS
+    vmem = pl.BlockSpec(memory_space=pltpu.VMEM)
+    hbm = pl.BlockSpec(memory_space=pl.ANY)
+    elements = chans * here_positions
+    return pl.pallas_call(
+        functools.partial(mix_kernel, nseq, nchan),
+        out_shape=jax.ShapeDtypeStruct((chans * nchan, here_positions // nchan), BF16),
+        in_specs=[hbm, hbm, vmem, vmem, vmem, vmem],
+        out_specs=hbm,
+        scratch_shapes=[
+            pltpu.VMEM((4, ROWS, here_positions), BF16),
+            pltpu.VMEM((2, ROWS, here, order), BF16),
+            pltpu.VMEM((2, nseq, ROWS, here, here), BF16),
+            pltpu.VMEM((3, nseq, ROWS, here, here), BF16),
+            pltpu.VMEM((2, nseq, here * ROWS, here), BF16),
+            pltpu.VMEM((3, nseq, here * ROWS, here), BF16),
+            pltpu.VMEM((2, nchan, ROWS, here_positions // nchan), BF16),
+            pltpu.VMEM((nseq * ROWS * ROWS, here), F32),
+            pltpu.VMEM((order * ROWS, here), F32),
+            pltpu.SemaphoreType.DMA((4,)),
+            pltpu.SemaphoreType.DMA((2,)),
+            pltpu.SemaphoreType.DMA((2, nseq)),
+            pltpu.SemaphoreType.DMA((3, nseq)),
+            pltpu.SemaphoreType.DMA((2, nseq)),
+            pltpu.SemaphoreType.DMA((3, nseq)),
+            pltpu.SemaphoreType.DMA((2, nchan)),
+            pltpu.SemaphoreType.DMA((chunks, nchan)),
+        ],
+        compiler_params=pltpu.CompilerParams(
+            collective_id=0, has_side_effects=True, vmem_limit_bytes=56 * 2**20
+        ),
+        cost_estimate=pl.CostEstimate(
+            flops=8 * elements * order, bytes_accessed=8 * elements, transcendentals=0
+        ),
+        name="mix",
+    )(inputs, kernel, forward_one, forward_two.T, inverse_two.T, inverse_one)
+
+
+SLOTS = 4
+TILE = 512
+
+
+def mlp_kernel(
+    nchan,
+    tok_ref,
+    gain_ref,
+    gate_ref,
+    up_ref,
+    down_ref,
+    out_hbm,
+    obuf,
+    normed,
+    total,
+    ssem,
+    rsem,
+):
+    t = pl.program_id(0)
+    steps = pl.num_programs(0)
+    me = lax.axis_index("chan")
+    width = tok_ref.shape[0] // nchan
+    held = out_hbm.shape[1] // nchan
+
+    def send(n, r):
+        to = lax.rem(me + r, nchan)
+        return pltpu.make_async_remote_copy(
+            src_ref=obuf.at[n % SLOTS, to],
+            dst_ref=out_hbm.at[:, pl.ds(me * held + n * TILE, TILE)],
+            send_sem=ssem.at[n % SLOTS, r],
+            recv_sem=rsem.at[n, r],
+            device_id={"chan": to},
+            device_id_type=MESH,
+        )
+
+    def arrived(n, r):
+        source = lax.rem(me + nchan - r, nchan)
+        return pltpu.make_async_remote_copy(
+            src_ref=obuf.at[n % SLOTS, source],
+            dst_ref=out_hbm.at[:, pl.ds(source * held + n * TILE, TILE)],
+            send_sem=ssem.at[n % SLOTS, r],
+            recv_sem=rsem.at[n, r],
+            device_id={"chan": source},
+            device_id_type=MESH,
+        )
+
+    def own(n):
+        return pltpu.make_async_copy(
+            obuf.at[n % SLOTS, me],
+            out_hbm.at[:, pl.ds(me * held + n * TILE, TILE)],
+            ssem.at[n % SLOTS, 0],
+        )
+
+    def wait_sent(n):
+        own(n).wait()
+        for r in range(1, nchan):
+            send(n, r).wait_send()
+
+    @pl.when(t == 0)
+    def _():
+        greet((("chan", nchan),))
+
+    x = tok_ref[...].astype(F32)
+    mean_square = jnp.mean(x * x, axis=0, keepdims=True)
+    normed[...] = (x * lax.rsqrt(mean_square + 1e-05) * gain_ref[...]).astype(BF16)
+    total[...] = x
+
+    def body(f, carry):
+        gate = jnp.dot(gate_ref[f], normed[...], preferred_element_type=F32)
+        up = jnp.dot(up_ref[f], normed[...], preferred_element_type=F32)
+        act = 0.5 * gate * (1.0 + jnp.tanh(0.7978845608 * (gate + 0.044715 * gate * gate * gate)))
+        hidden = (act * up).astype(BF16)
+        total[...] += jnp.dot(down_ref[f], hidden, preferred_element_type=F32)
+        return carry
+
+    lax.fori_loop(0, gate_ref.shape[0], body, 0)
+
+    @pl.when(t >= SLOTS)
+    def _():
+        wait_sent(t - SLOTS)
+
+    for d in range(nchan):
+        obuf[t % SLOTS, d] = total[d * width : (d + 1) * width, :].astype(BF16)
+    for r in range(1, nchan):
+        send(t, r).start()
+    own(t).start()
+
+    @pl.when(t == steps - 1)
+    def _():
+        def drain_sent(n, carry):
+            wait_sent(n)
+            return carry
+
+        lax.fori_loop(steps - SLOTS, steps, drain_sent, 0)
+
+        def drain(n, carry):
+            for r in range(1, nchan):
+                arrived(n, r).wait_recv()
+            return carry
+
+        lax.fori_loop(0, steps, drain, 0)
+
+
+def mlp(tokens, norm_gain, gate_rows, up_rows, down_rows, nchan):
+    width, held = tokens.shape
+    hidden = gate_rows.shape[0]
+    part = 256
+    parts = hidden // part
+    steps = held // TILE
+    gate_rows = gate_rows.reshape(parts, part, width)
+    up_rows = up_rows.reshape(parts, part, width)
+    down_rows = down_rows.reshape(parts, part, width).transpose(0, 2, 1)
+    whole = lambda *shape: pl.BlockSpec(shape, lambda t: (0,) * len(shape))
+    return pl.pallas_call(
+        functools.partial(mlp_kernel, nchan),
+        out_shape=jax.ShapeDtypeStruct((width // nchan, held * nchan), BF16),
+        grid=(steps,),
+        in_specs=[
+            pl.BlockSpec((width, TILE), lambda t: (0, t)),
+            whole(width, 1),
+            whole(parts, part, width),
+            whole(parts, part, width),
+            whole(parts, width, part),
+        ],
+        out_specs=pl.BlockSpec(memory_space=pl.ANY),
+        scratch_shapes=[
+            pltpu.VMEM((SLOTS, nchan, width // nchan, TILE), BF16),
+            pltpu.VMEM((width, TILE), BF16),
+            pltpu.VMEM((width, TILE), F32),
+            pltpu.SemaphoreType.DMA((SLOTS, nchan)),
+            pltpu.SemaphoreType.DMA((steps, nchan)),
+        ],
+        compiler_params=pltpu.CompilerParams(
+            collective_id=1,
+            has_side_effects=True,
+            vmem_limit_bytes=48 * 2**20,
+            dimension_semantics=("arbitrary",),
+        ),
+        cost_estimate=pl.CostEstimate(
+            flops=6 * width * hidden * held,
+            bytes_accessed=4 * width * held,
+            transcendentals=hidden * held,
+        ),
+        name="mlp",
+    )(tokens, norm_gain[:, None], gate_rows, up_rows, down_rows)
+
 
 def shards(
+    nseq,
+    nchan,
+    inputs,
+    kernel,
+    forward_one,
+    forward_two,
+    inverse_one,
+    inverse_two,
+    norm_gain,
+    w_gate,
+    w_up,
+    w_down,
+):
+    gate_rows = lax.all_gather(w_gate, "chan", axis=0, tiled=True)
+    up_rows = lax.all_gather(w_up, "chan", axis=0, tiled=True)
+    down_rows = lax.all_gather(w_down, "chan", axis=0, tiled=True)
+    tokens = mix(
+        inputs, kernel, forward_one, forward_two, inverse_one, inverse_two, nseq, nchan
+    )
+    return mlp(tokens, norm_gain, gate_rows, up_rows, down_rows, nchan)
+
+
+def plain_shards(
     inputs,
     kernel,
     forward_one,
@@ -59,8 +550,16 @@
 
 
 def solution(mesh):
+    nseq, nchan = mesh.shape["seq"], mesh.shape["chan"]
+
+    def body(inputs, kernel, forward_one, *rest):
+        here = forward_one.shape[0] // nseq
+        if here % 128 == 0 and here // nchan == ROWS and inputs.shape[0] % ROWS == 0:
+            return shards(nseq, nchan, inputs, kernel, forward_one, *rest)
+        return plain_shards(inputs, kernel, forward_one, *rest)
+
     return jax.shard_map(
-        shards,
+        body,
         mesh=mesh,
         in_specs=(
             P("chan", "seq"),

time: 1230 us -> 712 us (0.58)
  Pallas kernels: 0 us -> 673 us
  blocking collectives: 564 us -> 0 us
  waiting for transfers between devices: 338 us -> 2.11 us
  matrix products: 129 us -> 0 us
  local copies, waits for them, and re-layouts: 148 us -> 23 us
  other arithmetic: 19.8 us -> 0 us
    pallas_call x0 -> x2, Pallas kernels: none -> 673 us  [the longest x1 390 us: mix(): pl.pallas_call(functools.partial(mix_kernel, nseq, nchan), out_shape=jax....]
    all_to_all x3 -> x0, blocking collectives: 564 us -> none  [the longest x1 275 us: shards(): lax.all_to_all(result, 'chan', split_axis=0, concat_axis=1, tiled=True)]
    all_to_all x1 -> x0, waiting for transfers between devices: 306 us -> none  [shards(): lax.all_to_all(resid, 'chan', split_axis=1, concat_axis=0, tiled=True)]
    dot_general x5 -> x0, matrix products: 129 us -> none  [the longest x1 52.7 us: shards(): lax.dot_general(down_rows, hidden, (((0,), (0,)), ((), ())), preferred_el...]
    all_to_all x6 -> x0, local copies, waits for them, and re-layouts: 101 us -> none  [the longest x2 44.3 us: shards(): lax.all_to_all(partial_inv, 'seq', split_axis=2, concat_axis=1, tiled=True)]
    convert_element_type x2 -> x0, local copies, waits for them, and re-layouts: 33 us -> none  [the longest x1 16.5 us: shards(): first_section = jnp.einsum('cab,bk->cak', cube, forward_one, preferred_el...]
    all_gather x1, waiting for transfers between devices: 29.9 us -> 0.02 us  [shards(): down_rows = lax.all_gather(w_down, 'chan', axis=0, tiled=True)]
  transfers between devices with their start and end apart: 4 -> 3, of which waited for: 2 -> 0; matrix products, arithmetic and copies ran while one was open for 4% -> 1% of each run, Pallas kernels for 0% -> 55%
where the time goes in v1:
time: 712 us
  Pallas kernels  673 us (95%)
  local copies, waits for them, and re-layouts  23 us (3%)
  between operations  13.1 us (2%)
    pallas_call x1, Pallas kernels, mix(): pl.pallas_call(functools.partial(mix_kernel, nseq, nchan), out_shape=jax....  390 us
    pallas_call x1, Pallas kernels, mlp(): pl.pallas_call(functools.partial(mlp_kernel, nchan), out_shape=jax.ShapeD...  284 us
    unnamed x7, local copies, waits for them, and re-layouts  17.9 us
  transfers between devices with their start and end apart: 3, of which 0 were waited for; matrix products, arithmetic and copies ran while one was open for 1% of the time, Pallas kernels for 55%

profile of v1, /device:TPU:13, one launch (start us, length us, event | category | flops | bytes accessed | tf_op | source)
XLA Modules:
  0.0 711.7 jit_solution(3594596232965479140)
XLA Ops:
  6.5 0.0 all-gather.8.cloned.1.call-start
  6.5 0.7 all-gather.8.cloned.1.call-update
  7.3 0.0 all-gather.4.cloned.1.call-start
  7.3 0.7 all-gather.4.cloned.1.call-update
  8.0 0.0 all-gather.6.cloned.1.call-start
  8.1 0.7 all-gather.6.cloned.1.call-update
  8.7 0.8 broadcast_in_dim.4.gain_ref
  9.6 2.1 copy.13
  11.6 2.0 copy.14
  13.7 389.9 %mix.1.tok_ref = bf16[768,8192]{1,0:T(8,128)(2,1)} custom-call(bf16[96,65536]{1,0:T(8,128)(2,1)} %x_hbm.1, bf16[96,128,512]{2,1,0:T(8,128)(2,1)} %kern_hbm.1, bf16[512,512]{1,0:T(8,128)(2,1)} %f1_ref.1, bf16[512,512]{1,0:T(8,128)(2,1)} %bitcast.10, bf16[512,512]{1,0:T(8,128)(2,1)} %bitcast.11, bf16[512,512]{1,0:T(8,128)(2,1)} %i1_ref.1), custom_call_target="tpu_custom_call" | custom-call | flops 25769803776 | bytes 50331648 | tf_op jit(solution)/shard_map/mix/pallas_call | solution.py:294
  403.6 0.0 all-gather.8.cloned.1.call-done
  403.6 4.3 copy.15
  407.9 0.0 all-gather.4.cloned.1.call-done
  407.9 0.0 all-gather.6.cloned.1.call-done
  407.9 0.0 copy-start
  407.9 1.7 copy-done
  409.5 0.0 copy-start.1
  409.5 1.7 copy-done.1
  411.2 283.5 %mlp.1 = bf16[96,65536]{1,0:T(8,128)(2,1)} custom-call(bf16[768,8192]{1,0:T(8,128)(2,1)} %mix.1.tok_ref, f32[768,1]{1,0:T(8,128)S(1)} %broadcast_in_dim.4.gain_ref, bf16[6,256,768]{2,1,0:T(8,128)(2,1)S(1)} %bitcast.6, bf16[6,256,768]{2,1,0:T(8,128)(2,1)S(1)} %bitcast.7, bf16[6,768,256]{2,1,0:T(8,128)(2,1)} %bitcast.9), custom_call_target="tpu_custom_call" | custom-call | flops 57982058496 | bytes 25165824 | tf_op jit(solution)/shard_map/mlp/pallas_call | solution.py:441
  694.8 10.4 %copy.18 = bf16[96,65536]{1,0:T(8,128)(2,1)} copy(bf16[96,65536]{1,0:T(8,128)(2,1)} %mlp.1) | data formatting | bytes 25165824
Async XLA Ops:
  6.5 397.1 %all-gather.8.cloned.1.call-start = ((), (), s32[]{:S(2)}) async-start(), calls=%async_computation.2 | async-start | bytes 2654208 | tf_op jit(solution)/shard_map/all_gather | solution.py:491
  7.3 400.6 %all-gather.4.cloned.1.call-start = ((), (), s32[]{:S(2)}) async-start(), calls=%async_computation | async-start | bytes 2654208 | tf_op jit(solution)/shard_map/all_gather | solution.py:489
  8.0 399.9 %all-gather.6.cloned.1.call-start = ((), (), s32[]{:S(2)}) async-start(), calls=%async_computation.1 | async-start | bytes 2654208 | tf_op jit(solution)/shard_map/all_gather | solution.py:490
  407.9 1.7 copy-start
  409.5 1.7 copy-start.1
Sparse Core Ops, SparseCore 0:
  9.5 51.1 all-gather.7
  63.0 82.5 all-gather.3
  147.8 117.3 all-gather.5

commit v2 on v1

--- a/solution.py
+++ b/solution.py
@@ -11,6 +11,8 @@
 F32 = jnp.float32
 BF16 = jnp.bfloat16
 ROWS = 16
+TILE = 512
+SLOTS = 2
 
 
 def greet(peers):
@@ -27,16 +29,29 @@
     pl.semaphore_wait(barrier, sum(count - 1 for _, count in peers))
 
 
-def mix_kernel(
+def layer_kernel(
     nseq,
     nchan,
     x_hbm,
     kern_hbm,
     f1_ref,
+    f2_ref,
+    i2_ref,
+    i1_ref,
+    gain_ref,
+    gate_hbm,
+    up_hbm,
+    down_hbm,
+    tok_hbm,
+    out_hbm,
     f2t_ref,
     i2t_ref,
-    i1_ref,
-    tok_hbm,
+    wbuf,
+    downt,
+    tbuf,
+    obuf,
+    normed,
+    total,
     xbuf,
     kbuf,
     send1,
@@ -54,6 +69,13 @@
     r2sem,
     zssem,
     zrsem,
+    wlsem,
+    w1ssem,
+    w1rsem,
+    w23sem,
+    tsem,
+    ossem,
+    orsem,
 ):
     order = f1_ref.shape[0]
     here = order // nseq
@@ -145,6 +167,137 @@
             tok_hbm.at[pl.ds(me_c * chans + n * ROWS, ROWS), :],
             zssem.at[n % 2, 0],
         )
+
+    pairs = nchan // 2
+    zed, why = me_c // 2, me_c % 2
+    half = me_s % 2
+    mine = gate_hbm.shape[0] // 2
+    weights = (gate_hbm, up_hbm, down_hbm)
+
+    def w_own(j):
+        return pltpu.make_async_copy(
+            weights[j].at[pl.ds(half * mine, mine), :], wbuf.at[half, why, zed, j], wlsem.at[j]
+        )
+
+    def w_line(j, r):
+        return pltpu.make_async_remote_copy(
+            src_ref=weights[j].at[pl.ds(half * mine, mine), :],
+            dst_ref=wbuf.at[half, why, zed, j],
+            send_sem=w1ssem.at[j, r],
+            recv_sem=w1rsem.at[j, r],
+            device_id={"chan": lax.rem(zed + r, pairs) * 2 + why},
+            device_id_type=MESH,
+        )
+
+    def w_line_arrived(j, r):
+        source = lax.rem(zed + pairs - r, pairs)
+        return pltpu.make_async_remote_copy(
+            src_ref=weights[j].at[pl.ds(half * mine, mine), :],
+            dst_ref=wbuf.at[half, why, source, j],
+            send_sem=w1ssem.at[j, r],
+            recv_sem=w1rsem.at[j, r],
+            device_id={"chan": source * 2 + why},
+            device_id_type=MESH,
+        )
+
+    def w_pair(side):
+        return pltpu.make_async_remote_copy(
+            src_ref=wbuf.at[half, side],
+            dst_ref=wbuf.at[half, side],
+            send_sem=w23sem.at[0],
+            recv_sem=w23sem.at[1],
+            device_id={"chan": me_c + 1 - 2 * why},
+            device_id_type=MESH,
+        )
+
+    def w_cores(side):
+        return pltpu.make_async_remote_copy(
+            src_ref=wbuf.at[side],
+            dst_ref=wbuf.at[side],
+            send_sem=w23sem.at[2],
+            recv_sem=w23sem.at[3],
+            device_id={"seq": me_s + 1 - 2 * half},
+            device_id_type=MESH,
+        )
+
+    held = out_hbm.shape[1] // nchan
+    tiles = held // TILE
+
+    def load_tile(t):
+        return pltpu.make_async_copy(
+            tok_hbm.at[:, pl.ds(t * TILE, TILE)], tbuf.at[t % 2], tsem.at[t % 2]
+        )
+
+    def o_copy(t, r):
+        to = lax.rem(me_c + r, nchan)
+        return pltpu.make_async_remote_copy(
+            src_ref=obuf.at[t % SLOTS, to],
+            dst_ref=out_hbm.at[:, pl.ds(me_c * held + t * TILE, TILE)],
+            send_sem=ossem.at[t % SLOTS, r],
+            recv_sem=orsem.at[t, r],
+            device_id={"chan": to},
+            device_id_type=MESH,
+        )
+
+    def o_arrived(t, r):
+        source = lax.rem(me_c + nchan - r, nchan)
+        return pltpu.make_async_remote_copy(
+            src_ref=obuf.at[t % SLOTS, source],
+            dst_ref=out_hbm.at[:, pl.ds(source * held + t * TILE, TILE)],
+            send_sem=ossem.at[t % SLOTS, r],
+            recv_sem=orsem.at[t, r],
+            device_id={"chan": source},
+            device_id_type=MESH,
+        )
+
+    def o_own(t):
+        return pltpu.make_async_copy(
+            obuf.at[t % SLOTS, me_c],
+            out_hbm.at[:, pl.ds(me_c * held + t * TILE, TILE)],
+            ossem.at[t % SLOTS, 0],
+        )
+
+    def o_sent(t):
+        o_own(t).wait()
+        for r in range(1, nchan):
+            o_copy(t, r).wait_send()
+
+    def mlp_tile(t, carry):
+        @pl.when(t + 1 < tiles)
+        def _():
+            load_tile(t + 1).start()
+
+        load_tile(t).wait()
+        x = tbuf[t % 2].astype(F32)
+        mean_square = jnp.mean(x * x, axis=0, keepdims=True)
+        normed[...] = (x * lax.rsqrt(mean_square + 1e-05) * gain_ref[...]).astype(BF16)
+        total[...] = x
+
+        def body(f, carry):
+            h, y = f // 2, f % 2
+            gate_rows = jnp.concatenate([wbuf[h, y, z, 0] for z in range(pairs)], axis=0)
+            up_rows = jnp.concatenate([wbuf[h, y, z, 1] for z in range(pairs)], axis=0)
+            gate = jnp.dot(gate_rows, normed[...], preferred_element_type=F32)
+            up = jnp.dot(up_rows, normed[...], preferred_element_type=F32)
+            act = (
+                0.5 * gate * (1.0 + jnp.tanh(0.7978845608 * (gate + 0.044715 * gate * gate * gate)))
+            )
+            hidden = (act * up).astype(BF16)
+            total[...] += jnp.dot(downt[f], hidden, preferred_element_type=F32)
+            return carry
+
+        lax.fori_loop(0, 4, body, 0)
+
+        @pl.when(t >= SLOTS)
+        def _():
+            o_sent(t - SLOTS)
+
+        for d in range(nchan):
+            obuf[t % SLOTS, d] = total[d * chans : (d + 1) * chans, :].astype(BF16)
+        for r in range(1, nchan):
+            o_copy(t, r).start()
+        o_own(t).start()
+        return carry
 
     def stage_one(n):
         def body(g, carry):
@@ -227,9 +380,28 @@
         lax.fori_loop(0, nchan, body, 0)
 
     load_x(0).start()
+    f2t_ref[...] = f2_ref[...].astype(F32).T.astype(BF16)
+    i2t_ref[...] = i2_ref[...].astype(F32).T.astype(BF16)
     greet((("seq", nseq), ("chan", nchan)))
+    for j in range(3):
+        for r in range(1, pairs):
+            w_line(j, r).start()
+        w_own(j).start()
 
     def step(t, carry):
+        @pl.when(t == 2)
+        def _():
+            for j in range(3):
+                w_own(j).wait()
+                for r in range(1, pairs):
+                    w_line_arrived(j, r).wait_recv()
+            w_pair(why).start()
+
+        @pl.when(t == 4)
+        def _():
+            w_pair(1 - why).wait_recv()
+            w_cores(half).start()
+
         @pl.when(t < chunks)
         def _():
             @pl.when(t + 1 < chunks)
@@ -268,6 +440,16 @@
         return carry
 
     lax.fori_loop(0, chunks + 2, step, 0)
+    for j in range(3):
+        for r in range(1, pairs):
+            w_line(j, r).wait_send()
+    w_pair(why).wait_send()
+    w_cores(half).wait_send()
+    w_cores(1 - half).wait_recv()
+    for f in range(4):
+        rows = jnp.concatenate([wbuf[f // 2, f % 2, z, 2] for z in range(pairs)], axis=0)
+        downt[f] = rows.astype(F32).T.astype(BF16)
+
     for n in range(max(chunks - 2, 0), chunks):
         wait_sent(first, n)
         wait_sent(second, n)
@@ -281,195 +463,17 @@
         return carry
 
     lax.fori_loop(0, chunks, drain, 0)
-
-
-def mix(inputs, kernel, forward_one, forward_two, inverse_one, inverse_two, nseq, nchan):
-    chans, here_positions = inputs.shape
-    order = forward_one.shape[0]
-    here = order // nseq
-    chunks = chans // ROWS
-    vmem = pl.BlockSpec(memory_space=pltpu.VMEM)
-    hbm = pl.BlockSpec(memory_space=pl.ANY)
-    elements = chans * here_positions
-    return pl.pallas_call(
-        functools.partial(mix_kernel, nseq, nchan),
-        out_shape=jax.ShapeDtypeStruct((chans * nchan, here_positions // nchan), BF16),
-        in_specs=[hbm, hbm, vmem, vmem, vmem, vmem],
-        out_specs=hbm,
-        scratch_shapes=[
-            pltpu.VMEM((4, ROWS, here_positions), BF16),
-            pltpu.VMEM((2, ROWS, here, order), BF16),
-            pltpu.VMEM((2, nseq, ROWS, here, here), BF16),
-            pltpu.VMEM((3, nseq, ROWS, here, here), BF16),
-            pltpu.VMEM((2, nseq, here * ROWS, here), BF16),
-            pltpu.VMEM((3, nseq, here * ROWS, here), BF16),
-            pltpu.VMEM((2, nchan, ROWS, here_positions // nchan), BF16),
-            pltpu.VMEM((nseq * ROWS * ROWS, here), F32),
-            pltpu.VMEM((order * ROWS, here), F32),
-            pltpu.SemaphoreType.DMA((4,)),
-            pltpu.SemaphoreType.DMA((2,)),
-            pltpu.SemaphoreType.DMA((2, nseq)),
-            pltpu.SemaphoreType.DMA((3, nseq)),
-            pltpu.SemaphoreType.DMA((2, nseq)),
-            pltpu.SemaphoreType.DMA((3, nseq)),
-            pltpu.SemaphoreType.DMA((2, nchan)),
-            pltpu.SemaphoreType.DMA((chunks, nchan)),
-        ],
-        compiler_params=pltpu.CompilerParams(
-            collective_id=0, has_side_effects=True, vmem_limit_bytes=56 * 2**20
-        ),
-        cost_estimate=pl.CostEstimate(
-            flops=8 * elements * order, bytes_accessed=8 * elements, transcendentals=0
-        ),
-        name="mix",
-    )(inputs, kernel, forward_one, forward_two.T, inverse_two.T, inverse_one)
-
-
-SLOTS = 4
-TILE = 512
-
-
-def mlp_kernel(
-    nchan,
-    tok_ref,
-    gain_ref,
-    gate_ref,
-    up_ref,
-    down_ref,
-    out_hbm,
-    obuf,
-    normed,
-    total,
-    ssem,
-    rsem,
-):
-    t = pl.program_id(0)
-    steps = pl.num_programs(0)
-    me = lax.axis_index("chan")
-    width = tok_ref.shape[0] // nchan
-    held = out_hbm.shape[1] // nchan
-
-    def send(n, r):
-        to = lax.rem(me + r, nchan)
-        return pltpu.make_async_remote_copy(
-            src_ref=obuf.at[n % SLOTS, to],
-            dst_ref=out_hbm.at[:, pl.ds(me * held + n * TILE, TILE)],
-            send_sem=ssem.at[n % SLOTS, r],
-            recv_sem=rsem.at[n, r],
-            device_id={"chan": to},
-            device_id_type=MESH,
-        )
-
-    def arrived(n, r):
-        source = lax.rem(me + nchan - r, nchan)
-        return pltpu.make_async_remote_copy(
-            src_ref=obuf.at[n % SLOTS, source],
-            dst_ref=out_hbm.at[:, pl.ds(source * held + n * TILE, TILE)],
-            send_sem=ssem.at[n % SLOTS, r],
-            recv_sem=rsem.at[n, r],
-            device_id={"chan": source},
-            device_id_type=MESH,
-        )
-
-    def own(n):
-        return pltpu.make_async_copy(
-            obuf.at[n % SLOTS, me],
-            out_hbm.at[:, pl.ds(me * held + n * TILE, TILE)],
-            ssem.at[n % SLOTS, 0],
-        )
-
-    def wait_sent(n):
-        own(n).wait()
+    load_tile(0).start()
+    lax.fori_loop(0, tiles, mlp_tile, 0)
+    for t in range(tiles - SLOTS, tiles):
+        o_sent(t)
+
+    def drain_out(t, carry):
         for r in range(1, nchan):
-            send(n, r).wait_send()
-
-    @pl.when(t == 0)
-    def _():
-        greet((("chan", nchan),))
-
-    x = tok_ref[...].astype(F32)
-    mean_square = jnp.mean(x * x, axis=0, keepdims=True)
-    normed[...] = (x * lax.rsqrt(mean_square + 1e-05) * gain_ref[...]).astype(BF16)
-    total[...] = x
-
-    def body(f, carry):
-        gate = jnp.dot(gate_ref[f], normed[...], preferred_element_type=F32)
-        up = jnp.dot(up_ref[f], normed[...], preferred_element_type=F32)
-        act = 0.5 * gate * (1.0 + jnp.tanh(0.7978845608 * (gate + 0.044715 * gate * gate * gate)))
-        hidden = (act * up).astype(BF16)
-        total[...] += jnp.dot(down_ref[f], hidden, preferred_element_type=F32)
+            o_arrived(t, r).wait_recv()
         return carry
 
-    lax.fori_loop(0, gate_ref.shape[0], body, 0)
-
-    @pl.when(t >= SLOTS)
-    def _():
-        wait_sent(t - SLOTS)
-
-    for d in range(nchan):
-        obuf[t % SLOTS, d] = total[d * width : (d + 1) * width, :].astype(BF16)
-    for r in range(1, nchan):
-        send(t, r).start()
-    own(t).start()
-
-    @pl.when(t == steps - 1)
-    def _():
-        def drain_sent(n, carry):
-            wait_sent(n)
-            return carry
-
-        lax.fori_loop(steps - SLOTS, steps, drain_sent, 0)
-
-        def drain(n, carry):
-            for r in range(1, nchan):
-                arrived(n, r).wait_recv()
-            return carry
-
-        lax.fori_loop(0, steps, drain, 0)
-
-
-def mlp(tokens, norm_gain, gate_rows, up_rows, down_rows, nchan):
-    width, held = tokens.shape
-    hidden = gate_rows.shape[0]
-    part = 256
-    parts = hidden // part
-    steps = held // TILE
-    gate_rows = gate_rows.reshape(parts, part, width)
-    up_rows = up_rows.reshape(parts, part, width)
-    down_rows = down_rows.reshape(parts, part, width).transpose(0, 2, 1)
-    whole = lambda *shape: pl.BlockSpec(shape, lambda t: (0,) * len(shape))
-    return pl.pallas_call(
-        functools.partial(mlp_kernel, nchan),
-        out_shape=jax.ShapeDtypeStruct((width // nchan, held * nchan), BF16),
-        grid=(steps,),
-        in_specs=[
-            pl.BlockSpec((width, TILE), lambda t: (0, t)),
-            whole(width, 1),
-            whole(parts, part, width),
-            whole(parts, part, width),
-            whole(parts, width, part),
-        ],
-        out_specs=pl.BlockSpec(memory_space=pl.ANY),
-        scratch_shapes=[
-            pltpu.VMEM((SLOTS, nchan, width // nchan, TILE), BF16),
-            pltpu.VMEM((width, TILE), BF16),
-            pltpu.VMEM((width, TILE), F32),
-            pltpu.SemaphoreType.DMA((SLOTS, nchan)),
-            pltpu.SemaphoreType.DMA((steps, nchan)),
-        ],
-        compiler_params=pltpu.CompilerParams(
-            collective_id=1,
-            has_side_effects=True,
-            vmem_limit_bytes=48 * 2**20,
-            dimension_semantics=("arbitrary",),
-        ),
-        cost_estimate=pl.CostEstimate(
-            flops=6 * width * hidden * held,
-            bytes_accessed=4 * width * held,
-            transcendentals=hidden * held,
-        ),
-        name="mlp",
-    )(tokens, norm_gain[:, None], gate_rows, up_rows, down_rows)
+    lax.fori_loop(0, tiles, drain_out, 0)
 
 
 def shards(
@@ -486,13 +490,80 @@
     w_up,
     w_down,
 ):
-    gate_rows = lax.all_gather(w_gate, "chan", axis=0, tiled=True)
-    up_rows = lax.all_gather(w_up, "chan", axis=0, tiled=True)
-    down_rows = lax.all_gather(w_down, "chan", axis=0, tiled=True)
-    tokens = mix(
-        inputs, kernel, forward_one, forward_two, inverse_one, inverse_two, nseq, nchan
+    chans, positions = inputs.shape
+    order = forward_one.shape[0]
+    here = order // nseq
+    chunks = chans // ROWS
+    held = positions // nchan
+    width = chans * nchan
+    rows = w_gate.shape[0]
+    vmem = pl.BlockSpec(memory_space=pltpu.VMEM)
+    hbm = pl.BlockSpec(memory_space=pl.ANY)
+    elements = chans * positions
+    _, result = pl.pallas_call(
+        functools.partial(layer_kernel, nseq, nchan),
+        out_shape=[
+            jax.ShapeDtypeStruct((width, held), BF16),
+            jax.ShapeDtypeStruct((chans, positions), BF16),
+        ],
+        in_specs=[hbm, hbm, vmem, vmem, vmem, vmem, vmem, hbm, hbm, hbm],
+        out_specs=[hbm, hbm],
+        scratch_shapes=[
+            pltpu.VMEM((order, order), BF16),
+            pltpu.VMEM((order, order), BF16),
+            pltpu.VMEM((2, 2, nchan // 2, 3, rows // 2, width), BF16),
+            pltpu.VMEM((4, width, rows * nchan // 4), BF16),
+            pltpu.VMEM((2, width, TILE), BF16),
+            pltpu.VMEM((SLOTS, nchan, chans, TILE), BF16),
+            pltpu.VMEM((width, TILE), BF16),
+            pltpu.VMEM((width, TILE), F32),
+            pltpu.VMEM((4, ROWS, positions), BF16),
+            pltpu.VMEM((2, ROWS, here, order), BF16),
+            pltpu.VMEM((2, nseq, ROWS, here, here), BF16),
+            pltpu.VMEM((3, nseq, ROWS, here, here), BF16),
+            pltpu.VMEM((2, nseq, here * ROWS, here), BF16),
+            pltpu.VMEM((3, nseq, here * ROWS, here), BF16),
+            pltpu.VMEM((2, nchan, ROWS, held), BF16),
+            pltpu.VMEM((nseq * ROWS * ROWS, here), F32),
+            pltpu.VMEM((order * ROWS, here), F32),
+            pltpu.SemaphoreType.DMA((4,)),
+            pltpu.SemaphoreType.DMA((2,)),
+            pltpu.SemaphoreType.DMA((2, nseq)),
+            pltpu.SemaphoreType.DMA((3, nseq)),
+            pltpu.SemaphoreType.DMA((2, nseq)),
+            pltpu.SemaphoreType.DMA((3, nseq)),
+            pltpu.SemaphoreType.DMA((2, nchan)),
+            pltpu.SemaphoreType.DMA((chunks, nchan)),
+            pltpu.SemaphoreType.DMA((3,)),
+            pltpu.SemaphoreType.DMA((3, nchan // 2)),
+            pltpu.SemaphoreType.DMA((3, nchan // 2)),
+            pltpu.SemaphoreType.DMA((4,)),
+            pltpu.SemaphoreType.DMA((2,)),
+            pltpu.SemaphoreType.DMA((SLOTS, nchan)),
+            pltpu.SemaphoreType.DMA((held // TILE, nchan)),
+        ],
+        compiler_params=pltpu.CompilerParams(
+            collective_id=0, has_side_effects=True, vmem_limit_bytes=62 * 2**20
+        ),
+        cost_estimate=pl.CostEstimate(
+            flops=8 * elements * order + 6 * rows * nchan * elements,
+            bytes_accessed=12 * elements,
+            transcendentals=rows * elements // chans,
+        ),
+        name="layer",
+    )(
+        inputs,
+        kernel,
+        forward_one,
+        forward_two,
+        inverse_two,
+        inverse_one,
+        norm_gain[:, None],
+        w_gate,
+        w_up,
+        w_down,
     )
-    return mlp(tokens, norm_gain, gate_rows, up_rows, down_rows, nchan)
+    return result
 
 
 def plain_shards(
@@ -554,7 +625,9 @@
 
     def body(inputs, kernel, forward_one, *rest):
         here = forward_one.shape[0] // nseq
-        if here % 128 == 0 and here // nchan == ROWS and inputs.shape[0] % ROWS == 0:
+        fits = here % 128 == 0 and here // nchan == ROWS and inputs.shape[0] % ROWS == 0
+        fits = fits and nchan % 2 == 0 and rest[-1].shape[0] % 32 == 0
+        if fits and inputs.shape[0] >= 6 * ROWS:
             return shards(nseq, nchan, inputs, kernel, forward_one, *rest)
         return plain_shards(inputs, kernel, forward_one, *rest)
 

time: 712 us -> 634 us (0.89)
  Pallas kernels: 673 us -> 621 us
  between operations: 13.1 us -> 0.01 us
  local copies, waits for them, and re-layouts: 23 us -> 12 us
    pallas_call x2 -> x1, Pallas kernels: 673 us -> 621 us  [shards(): pl.pallas_call(functools.partial(layer_kernel, nseq, nchan), out_shape=[j...]
    unnamed x7 -> x1, local copies, waits for them, and re-layouts: 17.9 us -> 10.4 us
  transfers between devices with their start and end apart: 3 -> 0, of which waited for: 0 -> 0; matrix products, arithmetic and copies ran while one was open for 1% -> 0% of each run, Pallas kernels for 55% -> 0%
where the time goes in v2:
time: 634 us; the launch traced here: 633 us
  Pallas kernels  621 us (98%)
  local copies, waits for them, and re-layouts  12 us (2%)
    pallas_call x1, Pallas kernels, shards(): pl.pallas_call(functools.partial(layer_kernel, nseq, nchan), out_shape=[j...  621 us

profile of v2, /device:TPU:13, one launch (start us, length us, event | category | flops | bytes accessed | tf_op | source)
XLA Modules:
  0.0 633.2 jit_solution(3605976311097530523)
XLA Ops:
  0.0 1.6 broadcast_in_dim.4.gain_ref
  1.6 621.1 %layer.1 = (bf16[768,8192]{1,0:T(8,128)(2,1)}, bf16[96,65536]{1,0:T(8,128)(2,1)}) custom-call(bf16[96,65536]{1,0:T(8,128)(2,1)} %x_hbm.1, bf16[96,128,512]{2,1,0:T(8,128)(2,1)} %kern_hbm.1, bf16[512,512]{1,0:T(8,128)(2,1)} %f1_ref.1, bf16[512,512]{1,0:T(8,128)(2,1)} %f2_ref.1, bf16[512,512]{1,0:T(8,128)(2,1)} %i2_ref.1, bf16[512,512]{1,0:T(8,128)(2,1)} %i1_ref.1, ...), custom_call_target="tpu_custom_call" | custom-call | flops 83751862272 | bytes 75497472 | tf_op jit(solution)/shard_map/layer/pallas_call | solution.py:503
  622.7 10.4 %copy.13 = bf16[96,65536]{1,0:T(8,128)(2,1)} copy(bf16[96,65536]{1,0:T(8,128)(2,1)} %get-tuple-element.6) | data formatting | bytes 25165824

commit v3 on v2

--- a/solution.py
+++ b/solution.py
@@ -95,77 +95,128 @@
             kern_hbm.at[pl.ds(n * ROWS, ROWS)], kbuf.at[n % 2], ksem.at[n % 2]
         )
 
-    def across(send, recv, ssem, rsem, n, r):
+    def first_copy(n, r, part):
         to = lax.rem(me_s + r, nseq)
-        return pltpu.make_async_remote_copy(
-            src_ref=send.at[n % 2, to],
-            dst_ref=recv.at[n % 3, me_s],
-            send_sem=ssem.at[n % 2, r],
-            recv_sem=rsem.at[n % 3, r],
+        some = pl.ds(part * (ROWS // 2), ROWS // 2)
+        return pltpu.make_async_remote_copy(
+            src_ref=send1.at[n % 2, to, some],
+            dst_ref=recv1.at[n % 3, me_s, some],
+            send_sem=s1sem.at[n % 2, r, part],
+            recv_sem=r1sem.at[n % 3, r, part],
             device_id={"seq": to},
             device_id_type=MESH,
         )
 
-    def arrived(send, recv, ssem, rsem, n, r):
+    def first_arrived(n, r, part):
         source = lax.rem(me_s + nseq - r, nseq)
-        return pltpu.make_async_remote_copy(
-            src_ref=send.at[n % 2, source],
-            dst_ref=recv.at[n % 3, source],
-            send_sem=ssem.at[n % 2, r],
-            recv_sem=rsem.at[n % 3, r],
+        some = pl.ds(part * (ROWS // 2), ROWS // 2)
+        return pltpu.make_async_remote_copy(
+            src_ref=send1.at[n % 2, source, some],
+            dst_ref=recv1.at[n % 3, source, some],
+            send_sem=s1sem.at[n % 2, r, part],
+            recv_sem=r1sem.at[n % 3, r, part],
             device_id={"seq": source},
             device_id_type=MESH,
         )
 
-    def own(send, recv, ssem, n):
+    def first_own(n):
         return pltpu.make_async_copy(
-            send.at[n % 2, me_s], recv.at[n % 3, me_s], ssem.at[n % 2, 0]
-        )
-
-    first = (send1, recv1, s1sem, r1sem)
-    second = (send2, recv2, s2sem, r2sem)
-
-    def start_all(stage, n):
+            send1.at[n % 2, me_s], recv1.at[n % 3, me_s], s1sem.at[n % 2, 0, 0]
+        )
+
+    def start_first(n, part):
         for r in range(1, nseq):
-            across(*stage, n, r).start()
-        own(stage[0], stage[1], stage[2], n).start()
-
-    def wait_all(stage, n):
-        own(stage[0], stage[1], stage[2], n).wait()
+            first_copy(n, r, part).start()
+
+    def wait_first(n, part):
         for r in range(1, nseq):
-            arrived(*stage, n, r).wait_recv()
-
-    def wait_sent(stage, n):
-        for r in range(1, nseq):
-            across(*stage, n, r).wait_send()
-
-    def z_copy(n, r):
+            first_arrived(n, r, part).wait_recv()
+
+    def first_sent(n):
+        for part in range(2):
+            for r in range(1, nseq):
+                first_copy(n, r, part).wait_send()
+
+    def piece(z):
+        return pl.ds(lax.rem(me_c + z, nchan) * (per * ROWS), per * ROWS)
+
+    def second_copy(n, r, z):
+        to = lax.rem(me_s + r, nseq)
+        return pltpu.make_async_remote_copy(
+            src_ref=send2.at[n % 2, to, piece(z), :],
+            dst_ref=recv2.at[n % 3, me_s, piece(z), :],
+            send_sem=s2sem.at[n % 2, r, z],
+            recv_sem=r2sem.at[n % 3, r, z],
+            device_id={"seq": to},
+            device_id_type=MESH,
+        )
+
+    def second_arrived(n, r, z):
+        source = lax.rem(me_s + nseq - r, nseq)
+        return pltpu.make_async_remote_copy(
+            src_ref=send2.at[n % 2, source, piece(z), :],
+            dst_ref=recv2.at[n % 3, source, piece(z), :],
+            send_sem=s2sem.at[n % 2, r, z],
+            recv_sem=r2sem.at[n % 3, r, z],
+            device_id={"seq": source},
+            device_id_type=MESH,
+        )
+
+    def second_own(n):
+        return pltpu.make_async_copy(
+            send2.at[n % 2, me_s], recv2.at[n % 3, me_s], s2sem.at[n % 2, 0, 0]
+        )
+
+    def start_second(n):
+        second_own(n).start()
+
+        def body(step, carry):
+            for r in range(1, nseq):
+                second_copy(n, r, lax.rem(step + 1, nchan)).start()
+            return carry
+
+        lax.fori_loop(0, nchan, body, 0)
+
+    def second_sent(n):
+        def body(z, carry):
+            for r in range(1, nseq):
+                second_copy(n, r, z).wait_send()
+            return carry
+
+        lax.fori_loop(0, nchan, body, 0)
+
+    span = tok_hbm.shape[1] // 2
+
+    def z_copy(n, r, part):
         to = lax.rem(me_c + r, nchan)
-        return pltpu.make_async_remote_copy(
-            src_ref=zbuf.at[n % 2, to],
-            dst_ref=tok_hbm.at[pl.ds(me_c * chans + n * ROWS, ROWS), :],
-            send_sem=zssem.at[n % 2, r],
-            recv_sem=zrsem.at[n, r],
+        some = pl.ds(part * span, span)
+        return pltpu.make_async_remote_copy(
+            src_ref=zbuf.at[n % 2, to, :, some],
+            dst_ref=tok_hbm.at[pl.ds(me_c * chans + n * ROWS, ROWS), some],
+            send_sem=zssem.at[n % 2, r, part],
+            recv_sem=zrsem.at[n, r, part],
             device_id={"chan": to},
             device_id_type=MESH,
         )
 
-    def z_arrived(n, r):
+    def z_arrived(n, r, part):
         source = lax.rem(me_c + nchan - r, nchan)
-        return pltpu.make_async_remote_copy(
-            src_ref=zbuf.at[n % 2, source],
-            dst_ref=tok_hbm.at[pl.ds(source * chans + n * ROWS, ROWS), :],
-            send_sem=zssem.at[n % 2, r],
-            recv_sem=zrsem.at[n, r],
+        some = pl.ds(part * span, span)
+        return pltpu.make_async_remote_copy(
+            src_ref=zbuf.at[n % 2, source, :, some],
+            dst_ref=tok_hbm.at[pl.ds(source * chans + n * ROWS, ROWS), some],
+            send_sem=zssem.at[n % 2, r, part],
+            recv_sem=zrsem.at[n, r, part],
             device_id={"chan": source},
             device_id_type=MESH,
         )
 
-    def z_own(n):
+    def z_own(n, part):
+        some = pl.ds(part * span, span)
         return pltpu.make_async_copy(
-            zbuf.at[n % 2, me_c],
-            tok_hbm.at[pl.ds(me_c * chans + n * ROWS, ROWS), :],
-            zssem.at[n % 2, 0],
+            zbuf.at[n % 2, me_c, :, some],
+            tok_hbm.at[pl.ds(me_c * chans + n * ROWS, ROWS), some],
+            zssem.at[n % 2, 0, part],
         )
 
     pairs = nchan // 2
@@ -263,7 +314,7 @@
             o_copy(t, r).wait_send()
 
     def mlp_tile(t, carry):
-        @pl.when(t + 1 < tiles)
+        @pl.when(lax.rem(t + 1, tiles // 2) > 0)
         def _():
             load_tile(t + 1).start()
 
@@ -336,7 +387,10 @@
                 scr2[pl.ds(c + e, order, stride=ROWS), :] = inv[:, e * here : (e + 1) * here]
             return carry
 
-        lax.fori_loop(0, ROWS // 2, body, 0)
+        wait_first(n, 0)
+        lax.fori_loop(0, ROWS // 4, body, 0)
+        wait_first(n, 1)
+        lax.fori_loop(ROWS // 4, ROWS // 2, body, 0)
 
         def cast(d, carry):
             send2[n % 2, d] = scr2[pl.ds(d * (here * ROWS), here * ROWS), :].astype(BF16)
@@ -345,39 +399,52 @@
         lax.fori_loop(0, nseq, cast, 0)
 
     def stage_three(n):
+        some = per // 2
+
         def body(step, carry):
+            part = step // nchan
             r = lax.rem(step + 1, nchan)
             to = lax.rem(me_c + r, nchan)
 
+            @pl.when(part == 0)
+            def _():
+                for q in range(1, nseq):
+                    second_arrived(n, q, r).wait_recv()
+
             @pl.when(jnp.logical_and(n >= 2, r > 0))
             def _():
-                z_copy(n - 2, r).wait_send()
-
-            @pl.when(jnp.logical_and(n >= 2, r == 0))
-            def _():
-                z_own(n - 2).wait()
-
-            rows = pl.ds(to * (per * ROWS), per * ROWS)
+                z_copy(n - 2, r, part).wait_send()
+
+            rows = pl.ds((to * 2 + part) * (some * ROWS), some * ROWS)
             lhs = jnp.concatenate([recv2[n % 3, s, rows, :] for s in range(nseq)], axis=1)
             mixed = jnp.dot(lhs, i1_ref[...], preferred_element_type=F32)
-            x = xbuf[n % 4, :, pl.ds(to * (per * order), per * order)].astype(F32)
-            for i in range(per):
-                cols = slice(i * order, (i + 1) * order)
-                zbuf[n % 2, to, :, cols] = (
-                    x[:, cols] + mixed[i * ROWS : (i + 1) * ROWS]
-                ).astype(BF16)
+            x = xbuf[n % 4, :, pl.ds((to * 2 + part) * span, span)].astype(F32)
+            value = jnp.concatenate(
+                [
+                    x[:, i * order : (i + 1) * order] + mixed[i * ROWS : (i + 1) * ROWS]
+                    for i in range(some)
+                ],
+                axis=1,
+            )
+            zbuf[n % 2, to, :, pl.ds(part * span, span)] = value.astype(BF16)
 
             @pl.when(r > 0)
             def _():
-                z_copy(n, r).start()
+                z_copy(n, r, part).start()
 
             @pl.when(r == 0)
             def _():
-                z_own(n).start()
+                z_own(n, part).start()
 
             return carry
 
-        lax.fori_loop(0, nchan, body, 0)
+        @pl.when(n >= 2)
+        def _():
+            z_own(n - 2, 0).wait()
+            z_own(n - 2, 1).wait()
+
+        second_own(n).wait()
+        lax.fori_loop(0, 2 * nchan, body, 0)
 
     load_x(0).start()
     f2t_ref[...] = f2_ref[...].astype(F32).T.astype(BF16)
@@ -413,29 +480,32 @@
 
             @pl.when(t >= 2)
             def _():
-                wait_sent(first, t - 2)
+                first_sent(t - 2)
 
             stage_one(t)
-            start_all(first, t)
+            first_own(t).start()
+            start_first(t, 0)
+
+        @pl.when(t >= 2)
+        def _():
+            stage_three(t - 2)
 
         @pl.when(jnp.logical_and(t >= 1, t - 1 < chunks))
         def _():
             n = t - 1
             load_k(n).wait()
-            wait_all(first, n)
+            first_own(n).wait()
 
             @pl.when(n >= 2)
             def _():
-                wait_sent(second, n - 2)
+                second_sent(n - 2)
 
             stage_two(n)
-            start_all(second, n)
-
-        @pl.when(t >= 2)
-        def _():
-            n = t - 2
-            wait_all(second, n)
-            stage_three(n)
+            start_second(n)
+
+        @pl.when(t < chunks)
+        def _():
+            start_first(t, 1)
 
         return carry
 
@@ -450,21 +520,32 @@
         rows = jnp.concatenate([wbuf[f // 2, f % 2, z, 2] for z in range(pairs)], axis=0)
         downt[f] = rows.astype(F32).T.astype(BF16)
 
-    for n in range(max(chunks - 2, 0), chunks):
-        wait_sent(first, n)
-        wait_sent(second, n)
-        z_own(n).wait()
-        for r in range(1, nchan):
-            z_copy(n, r).wait_send()
-
-    def drain(n, carry):
-        for r in range(1, nchan):
-            z_arrived(n, r).wait_recv()
+    def mlp_part(part, carry):
+        def drain(n, carry):
+            for r in range(1, nchan):
+                z_arrived(n, r, part).wait_recv()
+            return carry
+
+        lax.fori_loop(0, chunks, drain, 0)
+
+        @pl.when(part == 0)
+        def _():
+            for n in range(chunks - 2, chunks):
+                z_own(n, 0).wait()
+                z_own(n, 1).wait()
+
+        load_tile(part * (tiles // 2)).start()
+        lax.fori_loop(part * (tiles // 2), (part + 1) * (tiles // 2), mlp_tile, 0)
         return carry
 
-    lax.fori_loop(0, chunks, drain, 0)
-    load_tile(0).start()
-    lax.fori_loop(0, tiles, mlp_tile, 0)
+    lax.fori_loop(0, 2, mlp_part, 0)
+    for n in range(chunks - 2, chunks):
+        first_sent(n)
+        second_sent(n)
+        for part in range(2):
+            for r in range(1, nchan):
+                z_copy(n, r, part).wait_send()
+
     for t in range(tiles - SLOTS, tiles):
         o_sent(t)
 
@@ -528,12 +609,12 @@
             pltpu.VMEM((order * ROWS, here), F32),
             pltpu.SemaphoreType.DMA((4,)),
             pltpu.SemaphoreType.DMA((2,)),
-            pltpu.SemaphoreType.DMA((2, nseq)),
-            pltpu.SemaphoreType.DMA((3, nseq)),
-            pltpu.SemaphoreType.DMA((2, nseq)),
-            pltpu.SemaphoreType.DMA((3, nseq)),
-            pltpu.SemaphoreType.DMA((2, nchan)),
-            pltpu.SemaphoreType.DMA((chunks, nchan)),
+            pltpu.SemaphoreType.DMA((2, nseq, 2)),
+            pltpu.SemaphoreType.DMA((3, nseq, 2)),
+            pltpu.SemaphoreType.DMA((2, nseq, nchan)),
+            pltpu.SemaphoreType.DMA((3, nseq, nchan)),
+            pltpu.SemaphoreType.DMA((2, nchan, 2)),
+            pltpu.SemaphoreType.DMA((chunks, nchan, 2)),
             pltpu.SemaphoreType.DMA((3,)),
             pltpu.SemaphoreType.DMA((3, nchan // 2)),
             pltpu.SemaphoreType.DMA((3, nchan // 2)),

time: 634 us -> 614 us (0.968)
  Pallas kernels: 621 us -> 602 us
    pallas_call x1, Pallas kernels: 621 us -> 602 us  [shards(): pl.pallas_call(functools.partial(layer_kernel, nseq, nchan), out_shape=[j...]
where the time goes in v3:
time: 614 us
  Pallas kernels  602 us (98%)
  local copies, waits for them, and re-layouts  12 us (2%)
    pallas_call x1, Pallas kernels, shards(): pl.pallas_call(functools.partial(layer_kernel, nseq, nchan), out_shape=[j...  602 us

profile of v3, /device:TPU:13, one launch (start us, length us, event | category | flops | bytes accessed | tf_op | source)
XLA Modules:
  0.0 614.2 jit_solution(4404474223531001418)
XLA Ops:
  0.0 1.6 broadcast_in_dim.4.gain_ref
  1.6 602.1 %layer.1 = (bf16[768,8192]{1,0:T(8,128)(2,1)}, bf16[96,65536]{1,0:T(8,128)(2,1)}) custom-call(bf16[96,65536]{1,0:T(8,128)(2,1)} %x_hbm.1, bf16[96,128,512]{2,1,0:T(8,128)(2,1)} %kern_hbm.1, bf16[512,512]{1,0:T(8,128)(2,1)} %f1_ref.1, bf16[512,512]{1,0:T(8,128)(2,1)} %f2_ref.1, bf16[512,512]{1,0:T(8,128)(2,1)} %i2_ref.1, bf16[512,512]{1,0:T(8,128)(2,1)} %i1_ref.1, ...), custom_call_target="tpu_custom_call" | custom-call | flops 83751862272 | bytes 75497472 | tf_op jit(solution)/shard_map/layer/pallas_call | solution.py:584
  603.7 10.4 %copy.13 = bf16[96,65536]{1,0:T(8,128)(2,1)} copy(bf16[96,65536]{1,0:T(8,128)(2,1)} %get-tuple-element.6) | data formatting | bytes 25165824
